TPU v7x, 32 devices: a whole 2x2x4 slice. The times are simulated.
32 devices in a mesh: sec: 2 (over core), gx: 4 (over z), gy: 4 (over y, x).
Axes of the slice: x: 2, y: 2, z: 4, core: 2. Of those that a mesh axis runs over, the one named last changes fastest.
Arguments:
- terminal: float32 [4, 16, 64, 1024], P('sec', None, 'gx', 'gy'), may hold values from -6 to 6
- forward_temp: bfloat16 [2, 4, 16, 64, 1024], P(None, 'sec', None, 'gx', 'gy'), may hold values from -6 to 6
- conductivity: float32 [16, 64, 1024], P(None, 'gx', 'gy'), may hold values from 0.02 to 0.15
- velocity: float32 [2, 16, 64, 1024], P(None, None, 'gx', 'gy'), may hold values from -0.3 to 0.3
- fixed_mask: int32 [16, 64, 1024], P(None, 'gx', 'gy'), may hold values 0 or 1
- wells: int32 [4, 8, 3], P('sec'), may hold values from 0 to 1023, as said below
- misfit: float32 [2, 4, 8], P(None, 'sec'), may hold values from -12 to 12
- head_gradient: bfloat16 [2, 16, 64, 1024], P('sec', None, 'gx', 'gy'), may hold values from -6 to 6
- blocks: bfloat16 [8, 7, 128, 128], P('gy'), may hold values from -0.1875 to 0.1875
- block_cols: int32 [8, 7], P('gy'), may hold values from 0 to 7, as said below
Outputs:
- head_adjoint: float32 [2, 16, 64, 1024], P('sec', None, 'gx', 'gy')
- sensitivity: float32 [16, 64, 1024], P(None, 'gx', 'gy')
Inputs may be any that keep to these rules, and one draw needn't show every extreme that they name: `wells`: each row is one cell (z, x, y) with z < 16, x < 64, y < 1024; the first test observes the cells (0, 0, 0) and (15, 63, 1023). `block_cols`: row r lists 7 different block columns, the first of which is r.
All inputs are finite; a program needn't handle non-finite values. No bound on the sum of `fixed_mask` on one device may be relied on, other than what follows from the above.
Results may differ from a plain program's by a relative error of at most 0.0029.
Values may be sent and summed in bfloat16 or wider, within the bound.
A program may use at most 64 MiB of HBM per device.

v0:
```python
import jax
import jax.numpy as jnp
from jax import lax
from jax.sharding import PartitionSpec as P


def extended(cells, sides, width):
    for axis, dim in sides:
        count = lax.axis_size(axis)
        ends = count - 1
        head = lax.slice_in_dim(cells, 0, width, axis=dim)
        tail = lax.slice_in_dim(cells, cells.shape[dim] - width, cells.shape[dim], axis=dim)
        cells = jnp.concatenate(
            [
                lax.ppermute(tail, axis, [(i, (i + 1) % count) for i in range(ends)]),
                cells,
                lax.ppermute(head, axis, [((i + 1) % count, i) for i in range(ends)]),
            ],
            axis=dim,
        )
    return cells


def shifted(padded):
    lead = [(0, 0)] * (padded.ndim - 3)
    deeper = jnp.pad(padded, lead + [(1, 1), (0, 0), (0, 0)])
    centre = deeper[..., 1:-1, 1:-1, 1:-1]
    beside_all = [
        deeper[..., 2:, 1:-1, 1:-1],
        deeper[..., :-2, 1:-1, 1:-1],
        deeper[..., 1:-1, 2:, 1:-1],
        deeper[..., 1:-1, :-2, 1:-1],
        deeper[..., 1:-1, 1:-1, 2:],
        deeper[..., 1:-1, 1:-1, :-2],
    ]
    return (centre, beside_all)


def face_weights(kappa_pad):
    centre, beside_all = shifted(kappa_pad)
    return [
        2.0 * centre * other / jnp.where(centre + other > 0.0, centre + other, 1.0)
        for other in beside_all
    ]


def advance(adjoint_pad, weights, keep, speed_x, speed_y, source):
    centre, beside_all = shifted(adjoint_pad)
    diffusion = weights[0] * (beside_all[0] - centre)
    for face in range(1, 6):
        diffusion = diffusion + weights[face] * (beside_all[face] - centre)
    slope_x = 0.5 * (beside_all[2] - beside_all[3])
    slope_y = 0.5 * (beside_all[4] - beside_all[5])
    updated = keep * (centre + diffusion + speed_x * slope_x + speed_y * slope_y + source)
    return (updated, diffusion, slope_x, slope_y)


def well_sources(wells, misfit_level, layers, rows_x, cols_y, margin):
    start_x = lax.axis_index("gx") * rows_x - margin
    start_y = lax.axis_index("gy") * cols_y - margin
    coord_z = jnp.arange(layers, dtype=jnp.int32)[:, None, None]
    coord_x = (start_x + jnp.arange(rows_x + 2 * margin, dtype=jnp.int32))[None, :, None]
    coord_y = (start_y + jnp.arange(cols_y + 2 * margin, dtype=jnp.int32))[None, None, :]
    well_z = wells[:, :, 0][:, :, None, None, None]
    well_x = wells[:, :, 1][:, :, None, None, None]
    well_y = wells[:, :, 2][:, :, None, None, None]
    matches = (coord_z == well_z) & (coord_x == well_x) & (coord_y == well_y)
    return jnp.sum(jnp.where(matches, misfit_level[:, :, None, None, None], 0.0), axis=1)


def shards(
    terminal,
    forward_temp,
    conductivity,
    velocity,
    fixed_mask,
    wells,
    misfit,
    head_gradient,
    blocks,
    block_cols,
):
    layers, rows_x, cols_y = conductivity.shape
    steps = forward_temp.shape[0]
    keep = 1.0 - fixed_mask.astype(jnp.float32)
    heat_sens = jnp.zeros((layers, rows_x, cols_y), jnp.float32)
    flow_x = jnp.zeros((layers, rows_x, cols_y), jnp.float32)
    flow_y = jnp.zeros((layers, rows_x, cols_y), jnp.float32)
    kappa_pad = extended(conductivity, (("gx", 1), ("gy", 2)), 1)
    weights = face_weights(kappa_pad)
    adjoint = terminal
    for level in reversed(range(steps)):
        padded = extended(adjoint, (("gx", 2), ("gy", 3)), 1)
        source = well_sources(wells, misfit[level], layers, rows_x, cols_y, 0)
        adjoint, diffusion, slope_x, slope_y = advance(
            padded, weights, keep, velocity[0], velocity[1], source
        )
        temper = forward_temp[level].astype(jnp.float32)
        heat_sens = heat_sens + jnp.sum(temper * diffusion, axis=0)
        flow_x = flow_x + jnp.sum(temper * slope_x, axis=0)
        flow_y = flow_y + jnp.sum(temper * slope_y, axis=0)
    summed = lax.psum_scatter(jnp.stack([flow_x, flow_y]), "sec", scatter_dimension=0, tiled=True)
    rounded = summed[0].astype(jnp.bfloat16)
    row_blocks, per_row, block_size, _ = blocks.shape
    piece = lax.all_gather(rounded, "gy", axis=2, tiled=True)
    count = piece.shape[2] // block_size
    split_rows = piece.reshape(layers, rows_x, count, block_size)
    block_ids = jnp.arange(count, dtype=jnp.int32)
    chosen = (block_cols[:, :, None] == block_ids[None, None, :]).astype(jnp.bfloat16)
    portion = jnp.einsum("bkq,zxqj->bkzxj", chosen, split_rows, preferred_element_type=jnp.float32)
    picked = portion.astype(jnp.bfloat16)
    head = jnp.einsum(
        "bkzxj,bkij->zxbi", picked, blocks, preferred_element_type=jnp.float32
    ).reshape(layers, rows_x, cols_y)
    partial_sens = heat_sens + head * head_gradient[0].astype(jnp.float32)
    sensitivity = lax.psum(partial_sens, "sec")
    return (head[None], sensitivity)


def solution(mesh):
    placed = (
        P("sec", None, "gx", "gy"),
        P(None, "sec", None, "gx", "gy"),
        P(None, "gx", "gy"),
        P(None, None, "gx", "gy"),
        P(None, "gx", "gy"),
        P("sec", None, None),
        P(None, "sec", None),
        P("sec", None, "gx", "gy"),
        P("gy", None, None, None),
        P("gy", None),
    )
    return jax.shard_map(
        shards,
        mesh=mesh,
        in_specs=placed,
        out_specs=(P("sec", None, "gx", "gy"), P(None, "gx", "gy")),
        check_vma=False,
    )
```

profile of v0, /device:TPU:0, one launch (start us, length us, event | category | flops | bytes accessed | tf_op | source)
XLA Modules:
  0.0 142.7 jit_solution(10783325855724493320)
XLA Ops:
  8.3 4.9 %collective-permute-start.2 = (f32[16,1,256]{2,1,0:T(1,128)S(1)}, f32[16,1,256]{2,1,0:T(1,128)S(1)}, u32[]{:S(2)}, u32[]{:S(2)}) collective-permute-start(f32[16,1,256]{2,1,0:T(1,128)S(1)} %get-tuple-element.29), channel_id=1, source_target_pairs={{0,4},{4,8},{8,12},{1,5},{5,9},{9,13},{2,6},{6,10},{10,14},{3,7},{... | collective-permute-start | bytes 49160 | tf_op jit(solution)/shard_map/ppermute | solution.py:15
  13.3 1.3 collective-permute-start.3
  15.6 1.3 collective-permute-start
  16.9 5.2 %collective-permute-start.1 = (f32[2,16,1,256]{3,2,1,0:T(1,128)S(1)}, f32[2,16,1,256]{3,2,1,0:T(1,128)S(1)}, u32[]{:S(2)}, u32[]{:S(2)}) collective-permute-start(f32[2,16,1,256]{3,2,1,0:T(1,128)S(1)} %get-tuple-element.20), channel_id=1, source_target_pairs={{0,4},{4,8},{8,12},{1,5},{5,9},{9,13},{2,6},{6,10},{10,14},{3,7},{... | collective-permute-start | bytes 98312 | tf_op jit(solution)/shard_map/ppermute | solution.py:15
  24.5 3.5 %collective-permute-start.4 = (f32[16,18,1]{2,1,0:T(8,128)S(1)}, f32[16,18,1]{2,1,0:T(8,128)S(1)}, u32[]{:S(2)}, u32[]{:S(2)}) collective-permute-start(f32[16,18,1]{2,1,0:T(8,128)S(1)} %get-tuple-element.22), channel_id=1, source_target_pairs={{0,1},{1,2},{2,3},{4,5},{5,6},{6,7},{8,9},{9,10},{10,11},{12,13},{... | collective-permute-start | bytes 3464 | tf_op jit(solution)/shard_map/ppermute | solution.py:15
  28.1 1.3 collective-permute-start.5
  30.2 1.2 collective-permute-done.4
  31.4 6.2 %collective-permute-done.5 = f32[16,18,1]{2,1,0:T(8,128)S(1)} collective-permute-done((f32[16,18,1]{2,1,0:T(8,128)S(1)}, f32[16,18,1]{2,1,0:T(8,128)S(1)}, u32[]{:S(2)}, u32[]{:S(2)}) %collective-permute-start.5) | collective-permute-done | bytes 1184 | tf_op jit(solution)/shard_map/ppermute | solution.py:17
  38.3 3.4 %collective-permute-start.6 = (f32[2,16,18,1]{3,2,1,0:T(8,128)S(1)}, f32[2,16,18,1]{3,2,1,0:T(8,128)S(1)}, u32[]{:S(2)}, u32[]{:S(2)}) collective-permute-start(f32[2,16,18,1]{3,2,1,0:T(8,128)S(1)} %get-tuple-element.14), channel_id=1, source_target_pairs={{0,1},{1,2},{2,3},{4,5},{5,6},{6,7},{8,9},{9,10},{10,11},{12,13},{... | collective-permute-start | bytes 6920 | tf_op jit(solution)/shard_map/ppermute | solution.py:15
  41.7 1.3 collective-permute-start.7
  43.6 5.6 %collective-permute-done.6 = f32[2,16,18,1]{3,2,1,0:T(8,128)S(1)} collective-permute-done((f32[2,16,18,1]{3,2,1,0:T(8,128)S(1)}, f32[2,16,18,1]{3,2,1,0:T(8,128)S(1)}, u32[]{:S(2)}, u32[]{:S(2)}) %collective-permute-start.6) | collective-permute-done | bytes 2336 | tf_op jit(solution)/shard_map/ppermute | solution.py:15
  49.2 9.2 %collective-permute-done.7 = f32[2,16,18,1]{3,2,1,0:T(8,128)S(1)} collective-permute-done((f32[2,16,18,1]{3,2,1,0:T(8,128)S(1)}, f32[2,16,18,1]{3,2,1,0:T(8,128)S(1)}, u32[]{:S(2)}, u32[]{:S(2)}) %collective-permute-start.7) | collective-permute-done | bytes 2336 | tf_op jit(solution)/shard_map/ppermute | solution.py:17
  60.2 1.3 collective-permute-start.8
  61.5 4.7 %collective-permute-start.9 = (f32[2,16,1,256]{3,2,1,0:T(1,128)S(1)}, f32[2,16,1,256]{3,2,1,0:T(1,128)S(1)}, u32[]{:S(2)}, u32[]{:S(2)}) collective-permute-start(f32[2,16,1,256]{3,2,1,0:T(1,128)S(1)} %get-tuple-element.16), channel_id=1, source_target_pairs={{0,4},{4,8},{8,12},{1,5},{5,9},{9,13},{2,6},{6,10},{10,14},{3,7},{... | collective-permute-start | bytes 98312 | tf_op jit(solution)/shard_map/ppermute | solution.py:15
  66.2 1.6 %collective-permute-done.9 = f32[2,16,1,256]{3,2,1,0:T(1,128)S(1)} collective-permute-done((f32[2,16,1,256]{3,2,1,0:T(1,128)S(1)}, f32[2,16,1,256]{3,2,1,0:T(1,128)S(1)}, u32[]{:S(2)}, u32[]{:S(2)}) %collective-permute-start.9) | collective-permute-done | bytes 32800 | tf_op jit(solution)/shard_map/ppermute | solution.py:15
  68.1 1.3 collective-permute-start.10
  69.4 4.6 %collective-permute-start.11 = (f32[2,16,18,1]{3,2,1,0:T(8,128)S(1)}, f32[2,16,18,1]{3,2,1,0:T(8,128)S(1)}, u32[]{:S(2)}, u32[]{:S(2)}) collective-permute-start(f32[2,16,18,1]{3,2,1,0:T(8,128)S(1)} %get-tuple-element.12), channel_id=1, source_target_pairs={{0,1},{1,2},{2,3},{4,5},{5,6},{6,7},{8,9},{9,10},{10,11},{12,13},{... | collective-permute-start | bytes 6920 | tf_op jit(solution)/shard_map/ppermute | solution.py:15
  74.6 7.4 %collective-permute-done.10 = f32[2,16,18,1]{3,2,1,0:T(8,128)S(1)} collective-permute-done((f32[2,16,18,1]{3,2,1,0:T(8,128)S(1)}, f32[2,16,18,1]{3,2,1,0:T(8,128)S(1)}, u32[]{:S(2)}, u32[]{:S(2)}) %collective-permute-start.10) | collective-permute-done | bytes 2336 | tf_op jit(solution)/shard_map/ppermute | solution.py:17
  82.0 1.3 fusion.7
  85.4 1.7 %fusion.9 = f32[16,16,256]{2,1,0:T(8,128)} fusion(f32[2,16,16,256]{3,2,1,0:T(8,128)S(1)} %get-tuple-element.7, f32[2,18,18,258]{3,2,1,0:T(8,128)S(1)} %select_maximum_fusion, f32[2,16,1,256]{3,2,1,0:T(1,128)S(1)} %collective-permute-done.9, f32[2,16,1,256]{3,2,1,0:T(1,128)S(1)} %collective-permute-done.8, f32[2,16,18,1]{3,2,1,0:T(8,128)S(1)} %collective-permute-done.10, ...), kind=kLoop, calls=%fused_computation.41 | loop fusion | flops 3604480 | bytes 3740160 | tf_op jit(solution)/shard_map/reduce_sum | solution.py:99
  87.0 10.6 %reduce-scatter.2.cloned.1.call-done = f32[1,16,16,256]{3,2,1,0:T(8,128)} async-done(((f32[2,16,16,256]{3,2,1,0:T(8,128)}), f32[1,16,16,256]{3,2,1,0:T(8,128)}) %reduce-scatter.2.cloned.1.call-update) | async-done | bytes 262160 | tf_op jit(solution)/shard_map/reduce_scatter | solution.py:102
  98.6 14.7 %all-gather = bf16[1,16,16,1024]{3,2,1,0:T(8,128)(2,1)S(1)} all-gather(bf16[1,16,16,256]{3,2,1,0:T(8,128)(2,1)S(1)} %convert_element_type.41), channel_id=2, replica_groups=mesh['sec'=2,'gx'=4,'gy'=4] {'gy'}, dimensions={3}, use_global_device_ids=true | all-gather | bytes 655360 | tf_op jit(solution)/shard_map/all_gather | solution.py:105
  116.9 17.3 %all-reduce.5.cloned.1.call-done = f32[16,16,256]{2,1,0:T(8,128)} async-done(((f32[16,16,256]{2,1,0:T(8,128)}), f32[16,16,256]{2,1,0:T(8,128)}) %all-reduce.5.cloned.1.call-update) | async-done | bytes 262160 | tf_op jit(solution)/shard_map/psum | solution.py:116
  134.2 1.7 %copy.26 = f32[16,16,256]{2,1,0:T(8,128)} copy(f32[16,16,256]{2,1,0:T(8,128)} %all-reduce.5.cloned.1.call-done) | data formatting | bytes 524288
  (67 shorter events, 15.9 us)
Async XLA Ops:
  7.2 106.8 %copy-start = (bf16[2,7,128,128]{3,2,1,0:T(8,128)(2,1)S(1)}, bf16[2,7,128,128]{3,2,1,0:T(8,128)(2,1)}, u32[]{:S(2)}) copy-start(bf16[2,7,128,128]{3,2,1,0:T(8,128)(2,1)} %param.18) | copy-start | bytes 1376260
  7.2 17.2 %copy-start.2 = (f32[16,16,256]{2,1,0:T(8,128)S(1)}, f32[16,16,256]{2,1,0:T(8,128)}, u32[]{:S(2)}) copy-start(f32[16,16,256]{2,1,0:T(8,128)} %param.12) | copy-start | bytes 786436
  7.2 16.8 %copy-start.7 = (s32[16,16,256]{2,1,0:T(8,128)S(1)}, s32[16,16,256]{2,1,0:T(8,128)}, u32[]{:S(2)}) copy-start(s32[16,16,256]{2,1,0:T(8,128)} %param.14) | copy-start | bytes 786436
  7.2 17.1 %copy-start.10 = (f32[2,2,8]{2,1,0:T(2,128)S(1)}, f32[2,2,8]{2,1,0:T(2,128)}, u32[]{:S(2)}) copy-start(f32[2,2,8]{2,1,0:T(2,128)} %param.16) | copy-start | bytes 388
  7.2 90.4 %reduce-scatter.2.cloned.1.call-start = ((), (), s32[]{:S(2)}) async-start(), calls=%async_computation.1 | async-start | bytes 786432 | tf_op jit(solution)/shard_map/reduce_scatter | solution.py:102
  8.3 16.0 %collective-permute-start.2 = (f32[16,1,256]{2,1,0:T(1,128)S(1)}, f32[16,1,256]{2,1,0:T(1,128)S(1)}, u32[]{:S(2)}, u32[]{:S(2)}) collective-permute-start(f32[16,1,256]{2,1,0:T(1,128)S(1)} %get-tuple-element.29), channel_id=1, source_target_pairs={{0,4},{4,8},{8,12},{1,5},{5,9},{9,13},{2,6},{6,10},{10,14},{3,7},{... | collective-permute-start | bytes 49160 | tf_op jit(solution)/shard_map/ppermute | solution.py:15
  13.3 11.1 %collective-permute-start.3 = (f32[16,1,256]{2,1,0:T(1,128)S(1)}, f32[16,1,256]{2,1,0:T(1,128)S(1)}, u32[]{:S(2)}, u32[]{:S(2)}) collective-permute-start(f32[16,1,256]{2,1,0:T(1,128)S(1)} %get-tuple-element.30), channel_id=1, source_target_pairs={{4,0},{8,4},{12,8},{5,1},{9,5},{13,9},{6,2},{10,6},{14,10},{7,3},{... | collective-permute-start | bytes 49160 | tf_op jit(solution)/shard_map/ppermute | solution.py:17
  15.6 22.3 %collective-permute-start = (f32[2,16,1,256]{3,2,1,0:T(1,128)S(1)}, f32[2,16,1,256]{3,2,1,0:T(1,128)S(1)}, u32[]{:S(2)}, u32[]{:S(2)}) collective-permute-start(f32[2,16,1,256]{3,2,1,0:T(1,128)S(1)} %get-tuple-element.19), channel_id=1, source_target_pairs={{4,0},{8,4},{12,8},{5,1},{9,5},{13,9},{6,2},{10,6},{14,10},{7,3},{... | collective-permute-start | bytes 98312 | tf_op jit(solution)/shard_map/ppermute | solution.py:17
  16.9 21.0 %collective-permute-start.1 = (f32[2,16,1,256]{3,2,1,0:T(1,128)S(1)}, f32[2,16,1,256]{3,2,1,0:T(1,128)S(1)}, u32[]{:S(2)}, u32[]{:S(2)}) collective-permute-start(f32[2,16,1,256]{3,2,1,0:T(1,128)S(1)} %get-tuple-element.20), channel_id=1, source_target_pairs={{0,4},{4,8},{8,12},{1,5},{5,9},{9,13},{2,6},{6,10},{10,14},{3,7},{... | collective-permute-start | bytes 98312 | tf_op jit(solution)/shard_map/ppermute | solution.py:15
  24.4 13.5 %copy-start.1 = (f32[2,16,16,256]{3,2,1,0:T(8,128)S(1)}, f32[2,16,16,256]{3,2,1,0:T(8,128)}, u32[]{:S(2)}) copy-start(f32[2,16,16,256]{3,2,1,0:T(8,128)} %param.10) | copy-start | bytes 1572868
  24.5 6.8 %collective-permute-start.4 = (f32[16,18,1]{2,1,0:T(8,128)S(1)}, f32[16,18,1]{2,1,0:T(8,128)S(1)}, u32[]{:S(2)}, u32[]{:S(2)}) collective-permute-start(f32[16,18,1]{2,1,0:T(8,128)S(1)} %get-tuple-element.22), channel_id=1, source_target_pairs={{0,1},{1,2},{2,3},{4,5},{5,6},{6,7},{8,9},{9,10},{10,11},{12,13},{... | collective-permute-start | bytes 3464 | tf_op jit(solution)/shard_map/ppermute | solution.py:15
  28.1 9.4 %collective-permute-start.5 = (f32[16,18,1]{2,1,0:T(8,128)S(1)}, f32[16,18,1]{2,1,0:T(8,128)S(1)}, u32[]{:S(2)}, u32[]{:S(2)}) collective-permute-start(f32[16,18,1]{2,1,0:T(8,128)S(1)} %get-tuple-element.21), channel_id=1, source_target_pairs={{1,0},{2,1},{3,2},{5,4},{6,5},{7,6},{9,8},{10,9},{11,10},{13,12},{... | collective-permute-start | bytes 3464 | tf_op jit(solution)/shard_map/ppermute | solution.py:17
  38.3 10.9 %collective-permute-start.6 = (f32[2,16,18,1]{3,2,1,0:T(8,128)S(1)}, f32[2,16,18,1]{3,2,1,0:T(8,128)S(1)}, u32[]{:S(2)}, u32[]{:S(2)}) collective-permute-start(f32[2,16,18,1]{3,2,1,0:T(8,128)S(1)} %get-tuple-element.14), channel_id=1, source_target_pairs={{0,1},{1,2},{2,3},{4,5},{5,6},{6,7},{8,9},{9,10},{10,11},{12,13},{... | collective-permute-start | bytes 6920 | tf_op jit(solution)/shard_map/ppermute | solution.py:15
  41.7 16.6 %collective-permute-start.7 = (f32[2,16,18,1]{3,2,1,0:T(8,128)S(1)}, f32[2,16,18,1]{3,2,1,0:T(8,128)S(1)}, u32[]{:S(2)}, u32[]{:S(2)}) collective-permute-start(f32[2,16,18,1]{3,2,1,0:T(8,128)S(1)} %get-tuple-element.13), channel_id=1, source_target_pairs={{1,0},{2,1},{3,2},{5,4},{6,5},{7,6},{9,8},{10,9},{11,10},{13,12},{... | collective-permute-start | bytes 6920 | tf_op jit(solution)/shard_map/ppermute | solution.py:17
  60.2 6.0 %collective-permute-start.8 = (f32[2,16,1,256]{3,2,1,0:T(1,128)S(1)}, f32[2,16,1,256]{3,2,1,0:T(1,128)S(1)}, u32[]{:S(2)}, u32[]{:S(2)}) collective-permute-start(f32[2,16,1,256]{3,2,1,0:T(1,128)S(1)} %get-tuple-element.15), channel_id=1, source_target_pairs={{4,0},{8,4},{12,8},{5,1},{9,5},{13,9},{6,2},{10,6},{14,10},{7,3},{... | collective-permute-start | bytes 98312 | tf_op jit(solution)/shard_map/ppermute | solution.py:17
  61.5 12.4 %copy-start.3 = (bf16[2,2,16,16,256]{4,3,2,1,0:T(8,128)(2,1)S(1)}, bf16[2,2,16,16,256]{4,3,2,1,0:T(8,128)(2,1)}, u32[]{:S(2)}) copy-start(bf16[2,2,16,16,256]{4,3,2,1,0:T(8,128)(2,1)} %param.11) | copy-start | bytes 1572868
  61.5 6.3 %collective-permute-start.9 = (f32[2,16,1,256]{3,2,1,0:T(1,128)S(1)}, f32[2,16,1,256]{3,2,1,0:T(1,128)S(1)}, u32[]{:S(2)}, u32[]{:S(2)}) collective-permute-start(f32[2,16,1,256]{3,2,1,0:T(1,128)S(1)} %get-tuple-element.16), channel_id=1, source_target_pairs={{0,4},{4,8},{8,12},{1,5},{5,9},{9,13},{2,6},{6,10},{10,14},{3,7},{... | collective-permute-start | bytes 98312 | tf_op jit(solution)/shard_map/ppermute | solution.py:15
  68.1 13.9 %collective-permute-start.10 = (f32[2,16,18,1]{3,2,1,0:T(8,128)S(1)}, f32[2,16,18,1]{3,2,1,0:T(8,128)S(1)}, u32[]{:S(2)}, u32[]{:S(2)}) collective-permute-start(f32[2,16,18,1]{3,2,1,0:T(8,128)S(1)} %get-tuple-element.11), channel_id=1, source_target_pairs={{1,0},{2,1},{3,2},{5,4},{6,5},{7,6},{9,8},{10,9},{11,10},{13,12},{... | collective-permute-start | bytes 6920 | tf_op jit(solution)/shard_map/ppermute | solution.py:17
  69.4 12.7 %collective-permute-start.11 = (f32[2,16,18,1]{3,2,1,0:T(8,128)S(1)}, f32[2,16,18,1]{3,2,1,0:T(8,128)S(1)}, u32[]{:S(2)}, u32[]{:S(2)}) collective-permute-start(f32[2,16,18,1]{3,2,1,0:T(8,128)S(1)} %get-tuple-element.12), channel_id=1, source_target_pairs={{0,1},{1,2},{2,3},{4,5},{5,6},{6,7},{8,9},{9,10},{10,11},{12,13},{... | collective-permute-start | bytes 6920 | tf_op jit(solution)/shard_map/ppermute | solution.py:15
  84.3 50.0 %all-reduce.5.cloned.1.call-start = ((), (), s32[]{:S(2)}) async-start(), calls=%async_computation.2 | async-start | bytes 524288 | tf_op jit(solution)/shard_map/psum | solution.py:116
  84.3 1.0 copy-start.4
  87.0 26.4 %copy-start.9 = (s32[2,7]{1,0:T(2,128)S(1)}, s32[2,7]{1,0:T(2,128)}, u32[]{:S(2)}) copy-start(s32[2,7]{1,0:T(2,128)} %param.19) | copy-start | bytes 172
  113.9 1.0 copy-start.6
  114.0 1.0 copy-start.8
  (1 other events, 1.0 us)
Sparse Core Ops, SparseCore 0:
  84.4 13.1 reduce-scatter.1
  115.9 18.2 all-reduce.4
where the time goes:
time: 143 us
  waiting for transfers between devices  59 us (41%)
  starting transfers between devices  34.1 us (24%)
  blocking collectives  14.7 us (10%)
  between operations  14.4 us (10%)
  other arithmetic  12.3 us (9%)
  local copies, waits for them, and re-layouts  7.21 us (5%)
    ppermute x6, starting transfers between devices, extended(): lax.ppermute(tail, axis, [(i, (i + 1) % count) for i in range(ends)])  26.3 us
    ppermute x6, waiting for transfers between devices, extended(): lax.ppermute(head, axis, [((i + 1) % count, i) for i in range(ends)])  22.8 us
    psum x1, waiting for transfers between devices, shards(): sensitivity = lax.psum(partial_sens, 'sec')  17.3 us
    all_gather x1, blocking collectives, shards(): piece = lax.all_gather(rounded, 'gy', axis=2, tiled=True)  14.7 us
    reduce_scatter x1, waiting for transfers between devices, shards(): lax.psum_scatter(jnp.stack([flow_x, flow_y]), 'sec', scatter_dimension=0,...  10.6 us
    ppermute x6, waiting for transfers between devices, extended(): lax.ppermute(tail, axis, [(i, (i + 1) % count) for i in range(ends)])  8.34 us
    ppermute x6, starting transfers between devices, extended(): lax.ppermute(head, axis, [((i + 1) % count, i) for i in range(ends)])  7.75 us
  transfers between devices with their start and end apart: 14, of which 8 were waited for; matrix products, arithmetic and copies ran while one was open for 7% of the time, Pallas kernels for 0%

commit v1 on v0

v1 whole, which is shorter than its diff:
```python
import functools

import jax
import jax.numpy as jnp
from jax import lax
from jax.experimental import pallas as pl
from jax.experimental.pallas import tpu as pltpu
from jax.sharding import PartitionSpec as P

MESH = pl.DeviceIdType.MESH
LANES = 128
CHUNKS = 4
NT = (((1,), (1,)), ((), ()))


def kernel(
    n_gx, n_gy, wells, misfit, cols, term, fwd, kappa, vel, mask, grad, blocks,
    head, sens, wgt, adj, heat, flow, flow_in, part, part_in,
    sx1, sy1, hx1, hy1, sx2, sy2, hx2, hy2,
    h_send, h_recv, f_send, f_recv, g_send, g_recv, p_send, p_recv, *gath,
):
    tests, layers, rows, width = term.shape
    row_blocks, per_row, size, _ = blocks.shape
    per = layers // CHUNKS
    s, gx, gy = lax.axis_index("sec"), lax.axis_index("gx"), lax.axis_index("gy")
    other = 1 - s
    exists = (gx > 0, gx < n_gx - 1, gy > 0, gy < n_gy - 1)
    target = (
        {"gx": jnp.maximum(gx - 1, 0)}, {"gx": jnp.minimum(gx + 1, n_gx - 1)},
        {"gy": jnp.maximum(gy - 1, 0)}, {"gy": jnp.minimum(gy + 1, n_gy - 1)},
    )

    row_id = lax.broadcasted_iota(jnp.int32, (rows, width), 0)
    col_id = lax.broadcasted_iota(jnp.int32, (rows, width), 1)
    lane = lax.broadcasted_iota(jnp.int32, (rows, LANES), 1)

    barrier = pltpu.get_barrier_semaphore()
    for side in (0, 1):
        @pl.when(exists[side])
        def _(side=side):
            pl.semaphore_signal(barrier, 1, device_id=target[side], device_id_type=MESH)
    for off in range(1, n_gy):
        pl.semaphore_signal(barrier, 1, device_id={"gy": lax.rem(gy + off, n_gy)}, device_id_type=MESH)
    pl.semaphore_signal(barrier, 1, device_id={"sec": other}, device_id_type=MESH)

    def halo(round_, side, sx, sy, hx, hy):
        opposite = side ^ 1
        src = sx.at[side] if side < 2 else sy.at[side - 2]
        dst = hx.at[opposite] if side < 2 else hy.at[opposite - 2]
        return pltpu.make_async_remote_copy(
            src_ref=src, dst_ref=dst,
            send_sem=h_send.at[round_, side], recv_sem=h_recv.at[round_, opposite],
            device_id=target[side], device_id_type=MESH,
        )

    def halo_recv(round_, side, sx, sy, hx, hy):
        src = sx.at[side] if side < 2 else sy.at[side - 2]
        dst = hx.at[side] if side < 2 else hy.at[side - 2]
        return pltpu.make_async_remote_copy(
            src_ref=src, dst_ref=dst,
            send_sem=h_send.at[round_, side], recv_sem=h_recv.at[round_, side],
            device_id=target[side], device_id_type=MESH,
        )

    def start_halo(round_, bufs):
        for side in range(4):
            @pl.when(exists[side])
            def _(side=side):
                halo(round_, side, *bufs).start()

    def wait_halo(round_, bufs):
        for side in range(4):
            @pl.when(exists[side])
            def _(side=side):
                halo_recv(round_, side, *bufs).wait()

            @pl.when(jnp.logical_not(exists[side]))
            def _(side=side):
                into = bufs[2].at[side] if side < 2 else bufs[3].at[side - 2]
                into[...] = jnp.zeros(into.shape, jnp.float32)

    zero = jnp.zeros((rows, LANES), jnp.float32)

    def pack1(z, carry):
        low, high = carry
        planes = [term[t, z] for t in range(tests)] + [kappa[z]]
        for slot, plane in enumerate(planes):
            here = lane == slot * layers + z
            low = jnp.where(here, plane[:, 0:1], low)
            high = jnp.where(here, plane[:, width - 1:width], high)
            sx1[0, slot, pl.ds(z, 1), :] = plane[0:1, :]
            sx1[1, slot, pl.ds(z, 1), :] = plane[rows - 1:rows, :]
        return low, high

    low, high = lax.fori_loop(0, layers, pack1, (zero, zero))
    sy1[0] = low
    sy1[1] = high
    expected = n_gy + (gx > 0).astype(jnp.int32) + (gx < n_gx - 1).astype(jnp.int32)
    pl.semaphore_wait(barrier, expected)
    bufs1 = (sx1, sy1, hx1, hy1)
    bufs2 = (sx2, sy2, hx2, hy2)
    start_halo(0, bufs1)

    cell = row_id * width + col_id
    plane_cells = rows * width
    marks = []
    for t in range(tests):
        for w in range(wells.shape[1]):
            lx = wells[t, w, 1] - gx * rows
            ly = wells[t, w, 2] - gy * width
            inside = (lx >= 0) & (lx < rows) & (ly >= 0) & (ly < width)
            place = wells[t, w, 0] * plane_cells + lx * width + ly
            marks.append(jnp.where(inside, place, -1))

    def sources(z, _):
        now = cell + z * plane_cells
        for t in range(tests):
            total = jnp.zeros((rows, width), jnp.float32)
            for w in range(wells.shape[1]):
                total = total + jnp.where(now == marks[t * wells.shape[1] + w], misfit[1, t, w], 0.0)
            adj[t, z] = total
        return 0

    lax.fori_loop(0, layers, sources, 0)
    wait_halo(0, bufs1)

    def picked_lane(ref, side, index):
        return jnp.sum(jnp.where(lane == index, ref[side], 0.0), axis=1, keepdims=True)

    def beside(plane, hx, hy, slot, z):
        xp = jnp.where(row_id == rows - 1, hx[1, slot, pl.ds(z, 1), :], pltpu.roll(plane, rows - 1, 0))
        xm = jnp.where(row_id == 0, hx[0, slot, pl.ds(z, 1), :], pltpu.roll(plane, 1, 0))
        index = slot * layers + z
        yp = jnp.where(col_id == width - 1, picked_lane(hy, 1, index), pltpu.roll(plane, width - 1, 1))
        ym = jnp.where(col_id == 0, picked_lane(hy, 0, index), pltpu.roll(plane, 1, 1))
        return xp, xm, yp, ym

    def harmonic(a, b):
        return 2.0 * a * b / (a + b)

    def first(z, carry):
        low, high = carry
        zp, zm = jnp.minimum(z + 1, layers - 1), jnp.maximum(z - 1, 0)
        k = kappa[z]
        weights = [harmonic(k, kappa[zp]), harmonic(k, kappa[zm])]
        weights += [harmonic(k, near) for near in beside(k, hx1, hy1, tests, z)]
        for face in range(6):
            wgt[face, z] = weights[face]
        keep = 1.0 - mask[z].astype(jnp.float32)
        hs = jnp.zeros((rows, width), jnp.float32)
        fx, fy = hs, hs
        for t in range(tests):
            c = term[t, z]
            near = (term[t, zp], term[t, zm]) + beside(c, hx1, hy1, t, z)
            diff = weights[0] * (near[0] - c)
            for face in range(1, 6):
                diff = diff + weights[face] * (near[face] - c)
            slope_x = 0.5 * (near[2] - near[3])
            slope_y = 0.5 * (near[4] - near[5])
            new = keep * (c + diff + vel[0, z] * slope_x + vel[1, z] * slope_y + adj[t, z])
            adj[t, z] = new
            here = lane == t * layers + z
            low = jnp.where(here, new[:, 0:1], low)
            high = jnp.where(here, new[:, width - 1:width], high)
            sx2[0, t, pl.ds(z, 1), :] = new[0:1, :]
            sx2[1, t, pl.ds(z, 1), :] = new[rows - 1:rows, :]
            temper = fwd[1, t, z].astype(jnp.float32)
            hs = hs + temper * diff
            fx = fx + temper * slope_x
            fy = fy + temper * slope_y
        heat[z] = hs
        flow[0, z] = fx
        flow[1, z] = fy
        return low, high

    low, high = lax.fori_loop(0, layers, first, (zero, zero))
    sy2[0] = low
    sy2[1] = high
    start_halo(1, bufs2)
    wait_halo(1, bufs2)

    def second(z, _):
        zp, zm = jnp.minimum(z + 1, layers - 1), jnp.maximum(z - 1, 0)
        hs, fx, fy = heat[z], flow[0, z], flow[1, z]
        for t in range(tests):
            c = adj[t, z]
            near = (adj[t, zp], adj[t, zm]) + beside(c, hx2, hy2, t, z)
            diff = wgt[0, z] * (near[0] - c)
            for face in range(1, 6):
                diff = diff + wgt[face, z] * (near[face] - c)
            temper = fwd[0, t, z].astype(jnp.float32)
            hs = hs + temper * diff
            fx = fx + temper * (0.5 * (near[2] - near[3]))
            fy = fy + temper * (0.5 * (near[4] - near[5]))
        heat[z] = hs
        flow[0, z] = fx
        flow[1, z] = fy
        return 0

    def span(c):
        return pl.ds(c * per, per)

    def flow_copy(c):
        return pltpu.make_async_remote_copy(
            src_ref=flow.at[other, span(c)], dst_ref=flow_in.at[span(c)],
            send_sem=f_send.at[c], recv_sem=f_recv.at[c],
            device_id={"sec": other}, device_id_type=MESH,
        )

    def part_copy(c):
        return pltpu.make_async_remote_copy(
            src_ref=part.at[span(c)], dst_ref=part_in.at[span(c)],
            send_sem=p_send.at[c], recv_sem=p_recv.at[c],
            device_id={"sec": other}, device_id_type=MESH,
        )

    mine = pl.ds(gy * row_blocks, row_blocks)

    def gather_copy(c, off):
        return pltpu.make_async_remote_copy(
            src_ref=gath[c].at[mine], dst_ref=gath[c].at[mine],
            send_sem=g_send.at[c, off - 1], recv_sem=g_recv.at[c, off - 1],
            device_id={"gy": lax.rem(gy + off, n_gy)}, device_id_type=MESH,
        )

    def gather_recv(c, off):
        theirs = pl.ds(lax.rem(gy + n_gy - off, n_gy) * row_blocks, row_blocks)
        return pltpu.make_async_remote_copy(
            src_ref=gath[c].at[mine], dst_ref=gath[c].at[theirs],
            send_sem=g_send.at[c, off - 1], recv_sem=g_recv.at[c, off - 1],
            device_id={"gy": lax.rem(gy + off, n_gy)}, device_id_type=MESH,
        )

    def spread(c):
        flow_copy(c).wait()
        total = (flow[s, span(c)] + flow_in[span(c)]).astype(jnp.bfloat16)
        for b in range(row_blocks):
            gath[c][gy * row_blocks + b] = total[:, :, b * size:(b + 1) * size]
        for off in range(1, n_gy):
            gather_copy(c, off).start()

    for c in range(CHUNKS):
        lax.fori_loop(c * per, (c + 1) * per, second, 0)
        flow_copy(c).start()
        if c > 0:
            spread(c - 1)
    spread(CHUNKS - 1)

    def finish(c):
        part_copy(c).wait()
        sens[span(c)] = part[span(c)] + part_in[span(c)]

    for c in range(CHUNKS):
        for off in range(1, n_gy):
            gather_recv(c, off).wait()
        for r in range(row_blocks):
            left = jnp.concatenate(
                [gath[c][cols[r, k]].reshape(per * rows, size) for k in range(per_row)], axis=1
            )
            right = jnp.concatenate([blocks[r, k] for k in range(per_row)], axis=1)
            out = lax.dot_general(left, right, NT, preferred_element_type=jnp.float32)
            out = out.reshape(per, rows, size)
            lanes = slice(r * size, (r + 1) * size)
            head[0, span(c), :, lanes] = out
            part[span(c), :, lanes] = heat[span(c), :, lanes] + out * grad[
                0, span(c), :, lanes
            ].astype(jnp.float32)
        part_copy(c).start()
        if c > 0:
            finish(c - 1)
    finish(CHUNKS - 1)


def solution(mesh):
    n_sec, n_gx, n_gy = (mesh.shape[a] for a in ("sec", "gx", "gy"))
    assert n_sec == 2

    def shards(
        terminal, forward_temp, conductivity, velocity, fixed_mask, wells, misfit, head_gradient,
        blocks, block_cols,
    ):
        tests, layers, rows, width = terminal.shape
        row_blocks, _, size, _ = blocks.shape
        field = (layers, rows, width)
        vmem = pl.BlockSpec(memory_space=pltpu.VMEM)
        smem = pl.BlockSpec(memory_space=pltpu.SMEM)
        f32 = jnp.float32
        dma = pltpu.SemaphoreType.DMA
        return pl.pallas_call(
            functools.partial(kernel, n_gx, n_gy),
            out_shape=(
                jax.ShapeDtypeStruct((1,) + field, f32),
                jax.ShapeDtypeStruct(field, f32),
            ),
            in_specs=[smem] * 3 + [vmem] * 7,
            out_specs=(vmem, vmem),
            scratch_shapes=[
                pltpu.VMEM((6,) + field, f32),
                pltpu.VMEM((tests,) + field, f32),
                pltpu.VMEM(field, f32),
                pltpu.VMEM((2,) + field, f32),
                pltpu.VMEM(field, f32),
                pltpu.VMEM(field, f32),
                pltpu.VMEM(field, f32),
                pltpu.VMEM((2, tests + 1, layers, width), f32),
                pltpu.VMEM((2, rows, LANES), f32),
                pltpu.VMEM((2, tests + 1, layers, width), f32),
                pltpu.VMEM((2, rows, LANES), f32),
                pltpu.VMEM((2, tests, layers, width), f32),
                pltpu.VMEM((2, rows, LANES), f32),
                pltpu.VMEM((2, tests, layers, width), f32),
                pltpu.VMEM((2, rows, LANES), f32),
                dma((2, 4)), dma((2, 4)),
                dma((CHUNKS,)), dma((CHUNKS,)),
                dma((CHUNKS, n_gy - 1)), dma((CHUNKS, n_gy - 1)),
                dma((CHUNKS,)), dma((CHUNKS,)),
            ] + [
                pltpu.VMEM((n_gy * row_blocks, layers // CHUNKS, rows, size), jnp.bfloat16)
                for _ in range(CHUNKS)
            ],
            compiler_params=pltpu.CompilerParams(
                collective_id=0, has_side_effects=True, vmem_limit_bytes=40 * 1024 * 1024
            ),
        )(
            wells, misfit, block_cols, terminal, forward_temp, conductivity, velocity, fixed_mask,
            head_gradient, blocks,
        )

    placed = (
        P("sec", None, "gx", "gy"),
        P(None, "sec", None, "gx", "gy"),
        P(None, "gx", "gy"),
        P(None, None, "gx", "gy"),
        P(None, "gx", "gy"),
        P("sec", None, None),
        P(None, "sec", None),
        P("sec", None, "gx", "gy"),
        P("gy", None, None, None),
        P("gy", None),
    )
    return jax.shard_map(
        shards,
        mesh=mesh,
        in_specs=placed,
        out_specs=(P("sec", None, "gx", "gy"), P(None, "gx", "gy")),
        check_vma=False,
    )
```

time: 143 us -> 37.2 us (0.26)
  waiting for transfers between devices: 59 us -> 0 us
  starting transfers between devices: 34.1 us -> 0 us
  Pallas kernels: 0 us -> 27 us
  blocking collectives: 14.7 us -> 0 us
  between operations: 14.4 us -> 0.66 us
  other arithmetic: 12.3 us -> 0 us
  local copies, waits for them, and re-layouts: 7.21 us -> 9.14 us
    ppermute x12 -> x0, starting transfers between devices: 34.1 us -> none  [the longest x6 26.3 us: extended(): lax.ppermute(tail, axis, [(i, (i + 1) % count) for i in range(ends)])]
    ppermute x12 -> x0, waiting for transfers between devices: 31.1 us -> none  [the longest x6 22.8 us: extended(): lax.ppermute(head, axis, [((i + 1) % count, i) for i in range(ends)])]
    pallas_call x0 -> x1, Pallas kernels: none -> 27 us  [shards(): pl.pallas_call(functools.partial(kernel, n_gx, n_gy), out_shape=(jax.Shap...]
    psum x1 -> x0, waiting for transfers between devices: 17.3 us -> none  [shards(): sensitivity = lax.psum(partial_sens, 'sec')]
    all_gather x1 -> x0, blocking collectives: 14.7 us -> none  [shards(): piece = lax.all_gather(rounded, 'gy', axis=2, tiled=True)]
    reduce_scatter x1 -> x0, waiting for transfers between devices: 10.6 us -> none  [shards(): lax.psum_scatter(jnp.stack([flow_x, flow_y]), 'sec', scatter_dimension=0,...]
    unnamed x24 -> x21, local copies, waits for them, and re-layouts: 2.74 us -> 9.14 us
    reduce_sum x4 -> x0, other arithmetic: 4.43 us -> none  [the longest x2 1.93 us: shards(): flow_x = flow_x + jnp.sum(temper * slope_x, axis=0)]
  transfers between devices with their start and end apart: 14 -> 0, of which waited for: 8 -> 0; matrix products, arithmetic and copies ran while one was open for 7% -> 0% of each run, Pallas kernels for 0% -> 0%
where the time goes in v1:
time: 37.2 us; the launch traced here: 36.8 us
  Pallas kernels  27 us (73%)
  local copies, waits for them, and re-layouts  9.14 us (25%)
  between operations  0.66 us (2%)
    pallas_call x1, Pallas kernels, shards(): pl.pallas_call(functools.partial(kernel, n_gx, n_gy), out_shape=(jax.Shap...  27 us
    unnamed x21, local copies, waits for them, and re-layouts  9.14 us

profile of v1, /device:TPU:0, one launch (start us, length us, event | category | flops | bytes accessed | tf_op | source)
XLA Modules:
  0.0 36.8 jit_solution(17556214738266623633)
XLA Ops:
  0.6 0.0 copy-start.8
  0.6 0.0 copy-start.7
  0.7 0.8 %copy.12.wells = s32[2,8,3]{2,1,0:T(8,128)S(1)} copy(s32[2,8,3]{1,0,2:T(2,128)} %param.15) | data formatting | bytes 384 | tf_op args[5]
  1.4 0.0 copy-done.8
  1.4 0.0 copy-done.7
  1.4 0.0 copy-start
  1.4 1.0 %copy-done = f32[2,16,16,256]{3,2,1,0:T(8,128)S(1)} copy-done((f32[2,16,16,256]{3,2,1,0:T(8,128)S(1)}, f32[2,16,16,256]{3,2,1,0:T(8,128)}, u32[]{:S(2)}) %copy-start) | copy-done | bytes 524312
  2.5 0.0 copy-start.1
  2.5 1.0 %copy-done.1 = bf16[2,2,16,16,256]{4,3,2,1,0:T(8,128)(2,1)S(1)} copy-done((bf16[2,2,16,16,256]{4,3,2,1,0:T(8,128)(2,1)S(1)}, bf16[2,2,16,16,256]{4,3,2,1,0:T(8,128)(2,1)}, u32[]{:S(2)}) %copy-start.1) | copy-done | bytes 524312
  3.5 0.0 copy-start.2
  3.5 1.0 %copy-done.2 = f32[2,16,16,256]{3,2,1,0:T(8,128)S(1)} copy-done((f32[2,16,16,256]{3,2,1,0:T(8,128)S(1)}, f32[2,16,16,256]{3,2,1,0:T(8,128)}, u32[]{:S(2)}) %copy-start.2) | copy-done | bytes 524312
  4.6 0.0 copy-start.3
  4.6 1.0 %copy-done.3 = bf16[2,7,128,128]{3,2,1,0:T(8,128)(2,1)S(1)} copy-done((bf16[2,7,128,128]{3,2,1,0:T(8,128)(2,1)S(1)}, bf16[2,7,128,128]{3,2,1,0:T(8,128)(2,1)}, u32[]{:S(2)}) %copy-start.3) | copy-done | bytes 458776
  5.6 0.0 copy-start.4
  5.6 0.9 %copy-done.4 = f32[16,16,256]{2,1,0:T(8,128)S(1)} copy-done((f32[16,16,256]{2,1,0:T(8,128)S(1)}, f32[16,16,256]{2,1,0:T(8,128)}, u32[]{:S(2)}) %copy-start.4) | copy-done | bytes 262168
  6.5 0.0 copy-start.5
  6.5 0.9 %copy-done.5 = s32[16,16,256]{2,1,0:T(8,128)S(1)} copy-done((s32[16,16,256]{2,1,0:T(8,128)S(1)}, s32[16,16,256]{2,1,0:T(8,128)}, u32[]{:S(2)}) %copy-start.5) | copy-done | bytes 262168
  7.5 0.0 copy-start.6
  7.5 0.9 %copy-done.6 = bf16[1,16,16,256]{3,2,1,0:T(8,128)(2,1)S(1)} copy-done((bf16[1,16,16,256]{3,2,1,0:T(8,128)(2,1)S(1)}, bf16[1,16,16,256]{3,2,1,0:T(8,128)(2,1)}, u32[]{:S(2)}) %copy-start.6) | copy-done | bytes 131096
  8.4 27.0 %shard_map.113 = (f32[1,16,16,256]{3,2,1,0:T(8,128)S(1)}, f32[16,16,256]{2,1,0:T(8,128)S(1)}) custom-call(s32[2,8,3]{2,1,0:T(8,128)S(1)} %copy.12.wells, f32[2,2,8]{2,1,0:T(2,128)S(1)} %copy-done.7, s32[2,7]{1,0:T(2,128)S(1)} %copy-done.8, f32[2,16,16,256]{3,2,1,0:T(8,128)S(1)} %copy-done, bf16[2,2,16,16,256]{4,3,2,1,0:T(8,128)(2,1)S(1)} %copy-done.1, ...), custom_call_target="tpu_custom_call" | custom-call | tf_op jit(solution)/shard_map/pallas_call | solution.py:289
  35.4 0.7 %copy.15 = f32[1,16,16,256]{3,2,1,0:T(8,128)} copy(f32[1,16,16,256]{3,2,1,0:T(8,128)S(1)} %get-tuple-element.4) | data formatting | bytes 524288
  36.1 0.7 %copy.16 = f32[16,16,256]{2,1,0:T(8,128)} copy(f32[16,16,256]{2,1,0:T(8,128)S(1)} %get-tuple-element.5) | data formatting | bytes 524288
Async XLA Ops:
  0.6 0.8 %copy-start.8 = (s32[2,7]{1,0:T(2,128)S(1)}, s32[2,7]{1,0:T(2,128)}, u32[]{:S(2)}) copy-start(s32[2,7]{1,0:T(2,128)} %cols.1) | copy-start | bytes 172
  0.6 0.8 %copy-start.7 = (f32[2,2,8]{2,1,0:T(2,128)S(1)}, f32[2,2,8]{2,1,0:T(2,128)}, u32[]{:S(2)}) copy-start(f32[2,2,8]{2,1,0:T(2,128)} %misfit.1) | copy-start | bytes 388
  1.4 1.0 %copy-start = (f32[2,16,16,256]{3,2,1,0:T(8,128)S(1)}, f32[2,16,16,256]{3,2,1,0:T(8,128)}, u32[]{:S(2)}) copy-start(f32[2,16,16,256]{3,2,1,0:T(8,128)} %term.1) | copy-start | bytes 1572868
  2.5 1.0 %copy-start.1 = (bf16[2,2,16,16,256]{4,3,2,1,0:T(8,128)(2,1)S(1)}, bf16[2,2,16,16,256]{4,3,2,1,0:T(8,128)(2,1)}, u32[]{:S(2)}) copy-start(bf16[2,2,16,16,256]{4,3,2,1,0:T(8,128)(2,1)} %fwd.1) | copy-start | bytes 1572868
  3.5 1.0 %copy-start.2 = (f32[2,16,16,256]{3,2,1,0:T(8,128)S(1)}, f32[2,16,16,256]{3,2,1,0:T(8,128)}, u32[]{:S(2)}) copy-start(f32[2,16,16,256]{3,2,1,0:T(8,128)} %vel.1) | copy-start | bytes 1572868
  4.6 1.0 %copy-start.3 = (bf16[2,7,128,128]{3,2,1,0:T(8,128)(2,1)S(1)}, bf16[2,7,128,128]{3,2,1,0:T(8,128)(2,1)}, u32[]{:S(2)}) copy-start(bf16[2,7,128,128]{3,2,1,0:T(8,128)(2,1)} %blocks.1) | copy-start | bytes 1376260
  5.6 0.9 %copy-start.4 = (f32[16,16,256]{2,1,0:T(8,128)S(1)}, f32[16,16,256]{2,1,0:T(8,128)}, u32[]{:S(2)}) copy-start(f32[16,16,256]{2,1,0:T(8,128)} %kappa.1) | copy-start | bytes 786436
  6.5 0.9 %copy-start.5 = (s32[16,16,256]{2,1,0:T(8,128)S(1)}, s32[16,16,256]{2,1,0:T(8,128)}, u32[]{:S(2)}) copy-start(s32[16,16,256]{2,1,0:T(8,128)} %mask.1) | copy-start | bytes 786436
  7.5 0.9 %copy-start.6 = (bf16[1,16,16,256]{3,2,1,0:T(8,128)(2,1)S(1)}, bf16[1,16,16,256]{3,2,1,0:T(8,128)(2,1)}, u32[]{:S(2)}) copy-start(bf16[1,16,16,256]{3,2,1,0:T(8,128)(2,1)} %grad.1) | copy-start | bytes 393220

commit v2 on v1

--- a/solution.py
+++ b/solution.py
@@ -14,8 +14,9 @@
 
 
 def kernel(
-    n_gx, n_gy, wells, misfit, cols, term, fwd, kappa, vel, mask, grad, blocks,
-    head, sens, wgt, adj, heat, flow, flow_in, part, part_in,
+    n_gx, n_gy, wells, misfit, cols,
+    term_in, fwd_in, kappa_in, vel_in, mask_in, grad_in, blocks_in, head, sens,
+    term, fwd, kappa, vel, mask, grad, blocks, in_sem, wgt, adj, heat, flow, flow_in, part, part_in,
     sx1, sy1, hx1, hy1, sx2, sy2, hx2, hy2,
     h_send, h_recv, f_send, f_recv, g_send, g_recv, p_send, p_recv, *gath,
 ):
@@ -34,6 +35,17 @@
     col_id = lax.broadcasted_iota(jnp.int32, (rows, width), 1)
     lane = lax.broadcasted_iota(jnp.int32, (rows, LANES), 1)
 
+    loads = {
+        name: pltpu.make_async_copy(src, dst, in_sem.at[i])
+        for i, (name, src, dst) in enumerate((
+            ("term", term_in, term), ("kappa", kappa_in, kappa), ("vel", vel_in, vel),
+            ("mask", mask_in, mask), ("fwd", fwd_in, fwd), ("grad", grad_in, grad),
+            ("blocks", blocks_in, blocks),
+        ))
+    }
+    for load in loads.values():
+        load.start()
+
     barrier = pltpu.get_barrier_semaphore()
     for side in (0, 1):
         @pl.when(exists[side])
@@ -78,6 +90,12 @@
             def _(side=side):
                 into = bufs[2].at[side] if side < 2 else bufs[3].at[side - 2]
                 into[...] = jnp.zeros(into.shape, jnp.float32)
+
+    def planes_of(lo, hi, body, carry):
+        def pair(i, carry):
+            return body(lo + 2 * i + 1, body(lo + 2 * i, carry))
+
+        return lax.fori_loop(0, (hi - lo) // 2, pair, carry)
 
     zero = jnp.zeros((rows, LANES), jnp.float32)
 
@@ -92,58 +110,64 @@
             sx1[1, slot, pl.ds(z, 1), :] = plane[rows - 1:rows, :]
         return low, high
 
-    low, high = lax.fori_loop(0, layers, pack1, (zero, zero))
+    loads["term"].wait()
+    loads["kappa"].wait()
+    low, high = planes_of(0, layers, pack1, (zero, zero))
     sy1[0] = low
     sy1[1] = high
     expected = n_gy + (gx > 0).astype(jnp.int32) + (gx < n_gx - 1).astype(jnp.int32)
     pl.semaphore_wait(barrier, expected)
     bufs1 = (sx1, sy1, hx1, hy1)
-    bufs2 = (sx2, sy2, hx2, hy2)
+    half = layers // 2
+    bufs2 = [tuple(ref.at[h] for ref in (sx2, sy2, hx2, hy2)) for h in range(2)]
     start_halo(0, bufs1)
 
     cell = row_id * width + col_id
     plane_cells = rows * width
     marks = []
     for t in range(tests):
-        for w in range(wells.shape[1]):
-            lx = wells[t, w, 1] - gx * rows
-            ly = wells[t, w, 2] - gy * width
+        for w in range(wells.shape[2]):
+            lx = wells[1, t, w] - gx * rows
+            ly = wells[2, t, w] - gy * width
             inside = (lx >= 0) & (lx < rows) & (ly >= 0) & (ly < width)
-            place = wells[t, w, 0] * plane_cells + lx * width + ly
+            place = wells[0, t, w] * plane_cells + lx * width + ly
             marks.append(jnp.where(inside, place, -1))
 
     def sources(z, _):
         now = cell + z * plane_cells
         for t in range(tests):
             total = jnp.zeros((rows, width), jnp.float32)
-            for w in range(wells.shape[1]):
-                total = total + jnp.where(now == marks[t * wells.shape[1] + w], misfit[1, t, w], 0.0)
+            for w in range(wells.shape[2]):
+                total = total + jnp.where(now == marks[t * wells.shape[2] + w], misfit[1, t, w], 0.0)
             adj[t, z] = total
         return 0
 
-    lax.fori_loop(0, layers, sources, 0)
+    planes_of(0, layers, sources, 0)
+    for name in ("vel", "mask", "fwd"):
+        loads[name].wait()
     wait_halo(0, bufs1)
 
-    def picked_lane(ref, side, index):
-        return jnp.sum(jnp.where(lane == index, ref[side], 0.0), axis=1, keepdims=True)
-
-    def beside(plane, hx, hy, slot, z):
+    def moved_lane(ref, side, shift):
+        return jnp.concatenate([pltpu.roll(ref[side], shift, 1)] * (width // LANES), axis=1)
+
+    def beside(plane, hx, hy, slot, z, depth):
         xp = jnp.where(row_id == rows - 1, hx[1, slot, pl.ds(z, 1), :], pltpu.roll(plane, rows - 1, 0))
         xm = jnp.where(row_id == 0, hx[0, slot, pl.ds(z, 1), :], pltpu.roll(plane, 1, 0))
-        index = slot * layers + z
-        yp = jnp.where(col_id == width - 1, picked_lane(hy, 1, index), pltpu.roll(plane, width - 1, 1))
-        ym = jnp.where(col_id == 0, picked_lane(hy, 0, index), pltpu.roll(plane, 1, 1))
+        index = slot * depth + z
+        up, down = LANES - 1 - index, lax.rem(LANES - index, LANES)
+        yp = jnp.where(col_id == width - 1, moved_lane(hy, 1, up), pltpu.roll(plane, width - 1, 1))
+        ym = jnp.where(col_id == 0, moved_lane(hy, 0, down), pltpu.roll(plane, 1, 1))
         return xp, xm, yp, ym
 
     def harmonic(a, b):
         return 2.0 * a * b / (a + b)
 
-    def first(z, carry):
+    def first(h, z, carry):
         low, high = carry
         zp, zm = jnp.minimum(z + 1, layers - 1), jnp.maximum(z - 1, 0)
         k = kappa[z]
         weights = [harmonic(k, kappa[zp]), harmonic(k, kappa[zm])]
-        weights += [harmonic(k, near) for near in beside(k, hx1, hy1, tests, z)]
+        weights += [harmonic(k, near) for near in beside(k, hx1, hy1, tests, z, layers)]
         for face in range(6):
             wgt[face, z] = weights[face]
         keep = 1.0 - mask[z].astype(jnp.float32)
@@ -151,7 +175,7 @@
         fx, fy = hs, hs
         for t in range(tests):
             c = term[t, z]
-            near = (term[t, zp], term[t, zm]) + beside(c, hx1, hy1, t, z)
+            near = (term[t, zp], term[t, zm]) + beside(c, hx1, hy1, t, z, layers)
             diff = weights[0] * (near[0] - c)
             for face in range(1, 6):
                 diff = diff + weights[face] * (near[face] - c)
@@ -159,11 +183,11 @@
             slope_y = 0.5 * (near[4] - near[5])
             new = keep * (c + diff + vel[0, z] * slope_x + vel[1, z] * slope_y + adj[t, z])
             adj[t, z] = new
-            here = lane == t * layers + z
+            here = lane == t * half + (z - h * half)
             low = jnp.where(here, new[:, 0:1], low)
             high = jnp.where(here, new[:, width - 1:width], high)
-            sx2[0, t, pl.ds(z, 1), :] = new[0:1, :]
-            sx2[1, t, pl.ds(z, 1), :] = new[rows - 1:rows, :]
+            sx2[h, 0, t, pl.ds(z - h * half, 1), :] = new[0:1, :]
+            sx2[h, 1, t, pl.ds(z - h * half, 1), :] = new[rows - 1:rows, :]
             temper = fwd[1, t, z].astype(jnp.float32)
             hs = hs + temper * diff
             fx = fx + temper * slope_x
@@ -173,18 +197,18 @@
         flow[1, z] = fy
         return low, high
 
-    low, high = lax.fori_loop(0, layers, first, (zero, zero))
-    sy2[0] = low
-    sy2[1] = high
-    start_halo(1, bufs2)
-    wait_halo(1, bufs2)
-
-    def second(z, _):
+    for h in range(2):
+        low, high = planes_of(h * half, (h + 1) * half, functools.partial(first, h), (zero, zero))
+        sy2[h, 0] = low
+        sy2[h, 1] = high
+        start_halo(1 + h, bufs2[h])
+
+    def second(h, z, _):
         zp, zm = jnp.minimum(z + 1, layers - 1), jnp.maximum(z - 1, 0)
         hs, fx, fy = heat[z], flow[0, z], flow[1, z]
         for t in range(tests):
             c = adj[t, z]
-            near = (adj[t, zp], adj[t, zm]) + beside(c, hx2, hy2, t, z)
+            near = (adj[t, zp], adj[t, zm]) + beside(c, hx2.at[h], hy2.at[h], t, z - h * half, half)
             diff = wgt[0, z] * (near[0] - c)
             for face in range(1, 6):
                 diff = diff + wgt[face, z] * (near[face] - c)
@@ -240,11 +264,17 @@
             gather_copy(c, off).start()
 
     for c in range(CHUNKS):
-        lax.fori_loop(c * per, (c + 1) * per, second, 0)
+        h = c // (CHUNKS // 2)
+        if c % (CHUNKS // 2) == 0:
+            wait_halo(1 + h, bufs2[h])
+        planes_of(c * per, (c + 1) * per, functools.partial(second, h), 0)
         flow_copy(c).start()
         if c > 0:
             spread(c - 1)
     spread(CHUNKS - 1)
+
+    loads["grad"].wait()
+    loads["blocks"].wait()
 
     def finish(c):
         part_copy(c).wait()
@@ -283,6 +313,7 @@
         row_blocks, _, size, _ = blocks.shape
         field = (layers, rows, width)
         vmem = pl.BlockSpec(memory_space=pltpu.VMEM)
+        hbm = pl.BlockSpec(memory_space=pltpu.HBM)
         smem = pl.BlockSpec(memory_space=pltpu.SMEM)
         f32 = jnp.float32
         dma = pltpu.SemaphoreType.DMA
@@ -292,9 +323,15 @@
                 jax.ShapeDtypeStruct((1,) + field, f32),
                 jax.ShapeDtypeStruct(field, f32),
             ),
-            in_specs=[smem] * 3 + [vmem] * 7,
+            in_specs=[smem] * 3 + [hbm] * 7,
             out_specs=(vmem, vmem),
             scratch_shapes=[
+                pltpu.VMEM(a.shape, a.dtype)
+                for a in (
+                    terminal, forward_temp, conductivity, velocity, fixed_mask, head_gradient, blocks
+                )
+            ] + [
+                dma((7,)),
                 pltpu.VMEM((6,) + field, f32),
                 pltpu.VMEM((tests,) + field, f32),
                 pltpu.VMEM(field, f32),
@@ -306,11 +343,11 @@
                 pltpu.VMEM((2, rows, LANES), f32),
                 pltpu.VMEM((2, tests + 1, layers, width), f32),
                 pltpu.VMEM((2, rows, LANES), f32),
-                pltpu.VMEM((2, tests, layers, width), f32),
-                pltpu.VMEM((2, rows, LANES), f32),
-                pltpu.VMEM((2, tests, layers, width), f32),
-                pltpu.VMEM((2, rows, LANES), f32),
-                dma((2, 4)), dma((2, 4)),
+                pltpu.VMEM((2, 2, tests, layers // 2, width), f32),
+                pltpu.VMEM((2, 2, rows, LANES), f32),
+                pltpu.VMEM((2, 2, tests, layers // 2, width), f32),
+                pltpu.VMEM((2, 2, rows, LANES), f32),
+                dma((3, 4)), dma((3, 4)),
                 dma((CHUNKS,)), dma((CHUNKS,)),
                 dma((CHUNKS, n_gy - 1)), dma((CHUNKS, n_gy - 1)),
                 dma((CHUNKS,)), dma((CHUNKS,)),
@@ -322,7 +359,7 @@
                 collective_id=0, has_side_effects=True, vmem_limit_bytes=40 * 1024 * 1024
             ),
         )(
-            wells, misfit, block_cols, terminal, forward_temp, conductivity, velocity, fixed_mask,
+            jnp.transpose(wells, (2, 0, 1)), misfit, block_cols, terminal, forward_temp, conductivity, velocity, fixed_mask,
             head_gradient, blocks,
         )
 

time: 37.2 us -> 35.5 us (0.954)
  Pallas kernels: 27 us -> 24 us
  local copies, waits for them, and re-layouts: 9.14 us -> 10.4 us
    pallas_call x1, Pallas kernels: 27 us -> 24 us  [shards(): pl.pallas_call(functools.partial(kernel, n_gx, n_gy), out_shape=(jax.Shap...]
    unnamed x21 -> x22, local copies, waits for them, and re-layouts: 9.14 us -> 10.4 us
where the time goes in v2:
time: 35.5 us; the launch traced here: 35.1 us
  Pallas kernels  24 us (68%)
  local copies, waits for them, and re-layouts  10.4 us (29%)
  between operations  0.66 us (2%)
    pallas_call x1, Pallas kernels, shards(): pl.pallas_call(functools.partial(kernel, n_gx, n_gy), out_shape=(jax.Shap...  24 us
    unnamed x22, local copies, waits for them, and re-layouts  10.4 us

profile of v2, /device:TPU:0, one launch (start us, length us, event | category | flops | bytes accessed | tf_op | source)
XLA Modules:
  0.0 35.1 jit_solution(11328229905886773753)
XLA Ops:
  0.6 0.0 copy-start.9
  0.6 0.7 %copy-done.9 = s32[2,7]{1,0:T(2,128)S(1)} copy-done((s32[2,7]{1,0:T(2,128)S(1)}, s32[2,7]{1,0:T(2,128)}, u32[]{:S(2)}) %copy-start.9) | copy-done | bytes 80
  1.3 0.0 copy-start
  1.3 1.0 %copy-done = f32[2,16,16,256]{3,2,1,0:T(8,128)S(1)} copy-done((f32[2,16,16,256]{3,2,1,0:T(8,128)S(1)}, f32[2,16,16,256]{3,2,1,0:T(8,128)}, u32[]{:S(2)}) %copy-start) | copy-done | bytes 524312
  2.4 0.0 copy-start.1
  2.4 1.0 %copy-done.1 = bf16[2,2,16,16,256]{4,3,2,1,0:T(8,128)(2,1)S(1)} copy-done((bf16[2,2,16,16,256]{4,3,2,1,0:T(8,128)(2,1)S(1)}, bf16[2,2,16,16,256]{4,3,2,1,0:T(8,128)(2,1)}, u32[]{:S(2)}) %copy-start.1) | copy-done | bytes 524312
  3.4 0.0 copy-start.2
  3.4 1.0 %copy-done.2 = f32[2,16,16,256]{3,2,1,0:T(8,128)S(1)} copy-done((f32[2,16,16,256]{3,2,1,0:T(8,128)S(1)}, f32[2,16,16,256]{3,2,1,0:T(8,128)}, u32[]{:S(2)}) %copy-start.2) | copy-done | bytes 524312
  4.4 0.0 copy-start.3
  4.4 1.0 %copy-done.3 = bf16[2,7,128,128]{3,2,1,0:T(8,128)(2,1)S(1)} copy-done((bf16[2,7,128,128]{3,2,1,0:T(8,128)(2,1)S(1)}, bf16[2,7,128,128]{3,2,1,0:T(8,128)(2,1)}, u32[]{:S(2)}) %copy-start.3) | copy-done | bytes 458776
  5.5 0.0 copy-start.4
  5.5 0.9 %copy-done.4 = f32[16,16,256]{2,1,0:T(8,128)S(1)} copy-done((f32[16,16,256]{2,1,0:T(8,128)S(1)}, f32[16,16,256]{2,1,0:T(8,128)}, u32[]{:S(2)}) %copy-start.4) | copy-done | bytes 262168
  6.4 0.0 copy-start.5
  6.4 0.9 %copy-done.5 = s32[16,16,256]{2,1,0:T(8,128)S(1)} copy-done((s32[16,16,256]{2,1,0:T(8,128)S(1)}, s32[16,16,256]{2,1,0:T(8,128)}, u32[]{:S(2)}) %copy-start.5) | copy-done | bytes 262168
  7.4 0.0 copy-start.6
  7.4 0.9 %copy-done.6 = bf16[1,16,16,256]{3,2,1,0:T(8,128)(2,1)S(1)} copy-done((bf16[1,16,16,256]{3,2,1,0:T(8,128)(2,1)S(1)}, bf16[1,16,16,256]{3,2,1,0:T(8,128)(2,1)}, u32[]{:S(2)}) %copy-start.6) | copy-done | bytes 131096
  8.3 0.0 copy-start.7
  8.3 0.7 %copy-done.7 = s32[2,8,3]{1,0,2:T(2,128)S(1)} copy-done((s32[2,8,3]{1,0,2:T(2,128)S(1)}, s32[2,8,3]{1,0,2:T(2,128)}, u32[]{:S(2)}) %copy-start.7) | copy-done | bytes 216
  8.9 0.0 copy-start.8
  9.0 0.7 %copy-done.8 = f32[2,2,8]{2,1,0:T(2,128)S(1)} copy-done((f32[2,2,8]{2,1,0:T(2,128)S(1)}, f32[2,2,8]{2,1,0:T(2,128)}, u32[]{:S(2)}) %copy-start.8) | copy-done | bytes 152
  9.6 24.0 %shard_map.113 = (f32[1,16,16,256]{3,2,1,0:T(8,128)S(1)}, f32[16,16,256]{2,1,0:T(8,128)S(1)}) custom-call(s32[3,2,8]{2,1,0:T(2,128)S(1)} %bitcast.1, f32[2,2,8]{2,1,0:T(2,128)S(1)} %copy-done.8, s32[2,7]{1,0:T(2,128)S(1)} %copy-done.9, f32[2,16,16,256]{3,2,1,0:T(8,128)S(1)} %copy-done, bf16[2,2,16,16,256]{4,3,2,1,0:T(8,128)(2,1)S(1)} %copy-done.1, ...), custom_call_target="tpu_custom_call" | custom-call | tf_op jit(solution)/shard_map/pallas_call | solution.py:320
  33.7 0.7 %copy.14 = f32[1,16,16,256]{3,2,1,0:T(8,128)} copy(f32[1,16,16,256]{3,2,1,0:T(8,128)S(1)} %get-tuple-element.4) | data formatting | bytes 524288
  34.4 0.7 %copy.15 = f32[16,16,256]{2,1,0:T(8,128)} copy(f32[16,16,256]{2,1,0:T(8,128)S(1)} %get-tuple-element.5) | data formatting | bytes 524288
Async XLA Ops:
  0.6 0.7 %copy-start.9 = (s32[2,7]{1,0:T(2,128)S(1)}, s32[2,7]{1,0:T(2,128)}, u32[]{:S(2)}) copy-start(s32[2,7]{1,0:T(2,128)} %cols.1) | copy-start | bytes 172
  1.3 1.0 %copy-start = (f32[2,16,16,256]{3,2,1,0:T(8,128)S(1)}, f32[2,16,16,256]{3,2,1,0:T(8,128)}, u32[]{:S(2)}) copy-start(f32[2,16,16,256]{3,2,1,0:T(8,128)} %term_in.1) | copy-start | bytes 1572868
  2.4 1.0 %copy-start.1 = (bf16[2,2,16,16,256]{4,3,2,1,0:T(8,128)(2,1)S(1)}, bf16[2,2,16,16,256]{4,3,2,1,0:T(8,128)(2,1)}, u32[]{:S(2)}) copy-start(bf16[2,2,16,16,256]{4,3,2,1,0:T(8,128)(2,1)} %fwd_in.1) | copy-start | bytes 1572868
  3.4 1.0 %copy-start.2 = (f32[2,16,16,256]{3,2,1,0:T(8,128)S(1)}, f32[2,16,16,256]{3,2,1,0:T(8,128)}, u32[]{:S(2)}) copy-start(f32[2,16,16,256]{3,2,1,0:T(8,128)} %vel_in.1) | copy-start | bytes 1572868
  4.4 1.0 %copy-start.3 = (bf16[2,7,128,128]{3,2,1,0:T(8,128)(2,1)S(1)}, bf16[2,7,128,128]{3,2,1,0:T(8,128)(2,1)}, u32[]{:S(2)}) copy-start(bf16[2,7,128,128]{3,2,1,0:T(8,128)(2,1)} %blocks_in.1) | copy-start | bytes 1376260
  5.5 0.9 %copy-start.4 = (f32[16,16,256]{2,1,0:T(8,128)S(1)}, f32[16,16,256]{2,1,0:T(8,128)}, u32[]{:S(2)}) copy-start(f32[16,16,256]{2,1,0:T(8,128)} %kappa_in.1) | copy-start | bytes 786436
  6.4 0.9 %copy-start.5 = (s32[16,16,256]{2,1,0:T(8,128)S(1)}, s32[16,16,256]{2,1,0:T(8,128)}, u32[]{:S(2)}) copy-start(s32[16,16,256]{2,1,0:T(8,128)} %mask_in.1) | copy-start | bytes 786436
  7.4 0.9 %copy-start.6 = (bf16[1,16,16,256]{3,2,1,0:T(8,128)(2,1)S(1)}, bf16[1,16,16,256]{3,2,1,0:T(8,128)(2,1)}, u32[]{:S(2)}) copy-start(bf16[1,16,16,256]{3,2,1,0:T(8,128)(2,1)} %grad_in.1) | copy-start | bytes 393220
  8.3 0.7 %copy-start.7 = (s32[2,8,3]{1,0,2:T(2,128)S(1)}, s32[2,8,3]{1,0,2:T(2,128)}, u32[]{:S(2)}) copy-start(s32[2,8,3]{1,0,2:T(2,128)} %param.15) | copy-start | bytes 580
  8.9 0.7 %copy-start.8 = (f32[2,2,8]{2,1,0:T(2,128)S(1)}, f32[2,2,8]{2,1,0:T(2,128)}, u32[]{:S(2)}) copy-start(f32[2,2,8]{2,1,0:T(2,128)} %misfit.1) | copy-start | bytes 388

commit v3 on v2

--- a/solution.py
+++ b/solution.py
@@ -356,7 +356,7 @@
                 for _ in range(CHUNKS)
             ],
             compiler_params=pltpu.CompilerParams(
-                collective_id=0, has_side_effects=True, vmem_limit_bytes=40 * 1024 * 1024
+                collective_id=0, has_side_effects=True, vmem_limit_bytes=62 * 1024 * 1024
             ),
         )(
             jnp.transpose(wells, (2, 0, 1)), misfit, block_cols, terminal, forward_temp, conductivity, velocity, fixed_mask,

time: 35.5 us -> 28 us (0.79)
  local copies, waits for them, and re-layouts: 10.4 us -> 2.42 us
  Pallas kernels: 24 us -> 24.7 us
    unnamed x22 -> x4, local copies, waits for them, and re-layouts: 10.4 us -> 2.42 us
    pallas_call x1, Pallas kernels: 24 us -> 24.7 us  [shards(): pl.pallas_call(functools.partial(kernel, n_gx, n_gy), out_shape=(jax.Shap...]
where the time goes in v3:
time: 28 us; the launch traced here: 27.8 us
  Pallas kernels  24.7 us (88%)
  local copies, waits for them, and re-layouts  2.42 us (9%)
  between operations  0.65 us (2%)
    pallas_call x1, Pallas kernels, shards(): pl.pallas_call(functools.partial(kernel, n_gx, n_gy), out_shape=(jax.Shap...  24.7 us
    unnamed x4, local copies, waits for them, and re-layouts  2.42 us

profile of v3, /device:TPU:0, one launch (start us, length us, event | category | flops | bytes accessed | tf_op | source)
XLA Modules:
  0.0 27.8 jit_solution(11738354724295844166)
XLA Ops:
  0.6 24.7 %shard_map.113 = (f32[1,16,16,256]{3,2,1,0:T(8,128)}, f32[16,16,256]{2,1,0:T(8,128)}) custom-call(s32[3,2,8]{2,1,0:T(2,128)} %bitcast.1, f32[2,2,8]{2,1,0:T(2,128)} %misfit.1, s32[2,7]{1,0:T(2,128)} %cols.1, f32[2,16,16,256]{3,2,1,0:T(8,128)} %term_in.1, bf16[2,2,16,16,256]{4,3,2,1,0:T(8,128)(2,1)} %fwd_in.1, f32[16,16,256]{2,1,0:T(8,128)} %kappa_in.1, ...), custom_call_target="tpu_custom_call" | custom-call | tf_op jit(solution)/shard_map/pallas_call | solution.py:320
  25.4 0.0 copy-start
  25.4 1.7 %copy.14 = f32[1,16,16,256]{3,2,1,0:T(8,128)} copy(f32[1,16,16,256]{3,2,1,0:T(8,128)} %get-tuple-element.4) | data formatting | bytes 524288
  27.1 0.0 copy-done
  27.1 0.7 %copy.15 = f32[16,16,256]{2,1,0:T(8,128)} copy(f32[16,16,256]{2,1,0:T(8,128)S(1)} %copy-done) | data formatting | bytes 524288
Async XLA Ops:
  25.4 1.7 %copy-start = (f32[16,16,256]{2,1,0:T(8,128)S(1)}, f32[16,16,256]{2,1,0:T(8,128)}, u32[]{:S(2)}) copy-start(f32[16,16,256]{2,1,0:T(8,128)} %get-tuple-element.5) | copy-start | bytes 786436
